TPU v7x, 256 devices: a whole 4x4x8 slice. The times are simulated.
256 devices in a mesh: store: 32 (over y, z), req: 4 (over x), tp: 2 (over core).
Axes of the slice: x: 4, y: 4, z: 8, core: 2. Of those that a mesh axis runs over, the one named last changes fastest.
Arguments:
- tokens: bfloat16 [16384, 8192], P(('store', 'req')), may hold values from -6 to 6
- queries: bfloat16 [16384, 8192], P(('store', 'req'), 'tp'), may hold values from -6 to 6
- plain_key_value: bfloat16 [16384, 2, 1024], P(('store', 'req'), None, 'tp'), may hold values from -6 to 6
- cached_key_value: bfloat16 [128, 2, 2048, 1024], P(('store', 'req'), None, None, 'tp'), may hold values from -6 to 6
- adapter_first_factor: bfloat16 [64, 8192, 128], P(None, ('store', 'tp')), may hold values from -0.0625 to 0.0625
- adapter_second_factor: bfloat16 [64, 2, 64, 1024], P('store', None, None, 'tp'), may hold values from -0.75 to 0.75
- request_adapter: int32 [128], P(('store', 'req')), may hold values from 0 to 63
- block_live_length: int32 [128], P(('store', 'req')), may hold values from 1 to 128, as said below
- context_length: int32 [128], P(('store', 'req')), may hold values from 0 to 2048, as said below
Outputs:
- new_kv: bfloat16 [16384, 2, 1024], P(('store', 'req'), None, 'tp')
- attention_out: bfloat16 [16384, 8192], P(('store', 'req'), 'tp')
Inputs may be any that keep to these rules, and one draw needn't show every extreme that they name: `request_adapter`: each request's adapter. The first block_live_length rows of a block are live, the rest padding. The first context_length cached positions of a request are live.
All inputs are finite; a program needn't handle non-finite values.
Results may differ from a plain program's by a relative error of at most 0.0086.
Values may be sent and summed in bfloat16 or wider, within the bound.
A program may use at most 128 MiB of HBM per device.

v0:
```python
import math

import jax
import jax.numpy as jnp
from jax import lax
from jax.sharding import PartitionSpec as P

HEAD_WIDTH = 128


def rotate_keys(key_heads, positions):
    half_size = key_heads.shape[-1] // 2
    index_float = jnp.arange(half_size).astype(jnp.float32)
    frequency = 10000.0 ** (-2.0 * index_float / key_heads.shape[-1])
    angles = positions.astype(jnp.float32)[:, None] * frequency[None, :]
    cosine = jnp.cos(angles)[:, None, :]
    sine_part = jnp.sin(angles)[:, None, :]
    first_half = key_heads[..., :half_size]
    second_half = key_heads[..., half_size:]
    return jnp.concatenate(
        [
            first_half * cosine - second_half * sine_part,
            second_half * cosine + first_half * sine_part,
        ],
        axis=-1,
    )


def attend_block(queries, cached_key_value, new_rows, live_rows, context_len):
    row_count = queries.shape[0]
    key_value_width = new_rows.shape[2]
    kv_heads = key_value_width // HEAD_WIDTH
    group_size = queries.shape[1] // key_value_width
    context = cached_key_value.shape[2]
    score_scale = 1.0 / math.sqrt(HEAD_WIDTH)
    query_heads = jnp.moveaxis(queries.reshape(row_count, kv_heads, group_size, HEAD_WIDTH), 1, 0)
    old_keys = jnp.moveaxis(cached_key_value[0, 0].reshape(context, kv_heads, HEAD_WIDTH), 1, 0)
    old_values = jnp.moveaxis(cached_key_value[0, 1].reshape(context, kv_heads, HEAD_WIDTH), 1, 0)
    new_keys = jnp.moveaxis(new_rows[:, 0].reshape(row_count, kv_heads, HEAD_WIDTH), 1, 0)
    new_values = jnp.moveaxis(new_rows[:, 1].reshape(row_count, kv_heads, HEAD_WIDTH), 1, 0)
    positions = jnp.arange(row_count)
    old_mask = (jnp.arange(context) < context_len)[None, None, :]
    new_mask = ((positions[None, :] <= positions[:, None]) & live_rows[None, :])[None]

    def one_head(head_items):
        query_rows, keys_old, values_old, keys_new, values_new = head_items
        score_old = (
            jnp.einsum("igd,jd->gij", query_rows, keys_old, preferred_element_type=jnp.float32)
            * score_scale
        )
        score_new = (
            jnp.einsum("igd,jd->gij", query_rows, keys_new, preferred_element_type=jnp.float32)
            * score_scale
        )
        score_old = jnp.where(old_mask, score_old, -jnp.inf)
        score_new = jnp.where(new_mask, score_new, -jnp.inf)
        highest = jnp.maximum(score_old.max(-1), score_new.max(-1))[..., None]
        exp_old = jnp.exp(score_old - highest)
        exp_new = jnp.exp(score_new - highest)
        denominator = exp_old.sum(-1, keepdims=True) + exp_new.sum(-1, keepdims=True)
        weight_old = (exp_old / denominator).astype(jnp.bfloat16)
        weight_new = (exp_new / denominator).astype(jnp.bfloat16)
        attended = jnp.einsum(
            "gij,jd->igd", weight_old, values_old, preferred_element_type=jnp.float32
        )
        return attended + jnp.einsum(
            "gij,jd->igd", weight_new, values_new, preferred_element_type=jnp.float32
        )

    attended = lax.map(one_head, (query_heads, old_keys, old_values, new_keys, new_values))
    merged = jnp.moveaxis(attended, 0, 1).reshape(row_count, -1)
    return jnp.where(live_rows[:, None], merged, 0.0).astype(jnp.bfloat16)


def shards(
    tokens,
    queries,
    plain_key_value,
    cached_key_value,
    adapter_first_factor,
    adapter_second_factor,
    request_adapter,
    block_live_length,
    context_length,
):
    store_count = lax.axis_size("store")
    tp_count = lax.axis_size("tp")
    row_count = tokens.shape[0]
    feature_total = adapter_first_factor.shape[1]
    tp_index = lax.axis_index("tp")
    split_rows = tokens.reshape(row_count, store_count, tp_count, feature_total)
    own_half = lax.dynamic_index_in_dim(split_rows, tp_index, axis=2, keepdims=False)
    id_slots = jnp.broadcast_to(request_adapter.reshape(1, 1, 1), (1, store_count, 1))
    arrived, arrived_ids = (
        lax.all_to_all(own_half, "store", split_axis=1, concat_axis=0, tiled=True),
        lax.all_to_all(id_slots, "store", split_axis=1, concat_axis=0, tiled=True),
    )
    flat_rows = arrived.reshape(store_count * row_count, feature_total)
    source_index = arrived_ids.reshape(store_count)
    selected_first_factor = jnp.take(adapter_first_factor, source_index, axis=0)
    block_count = row_count * lax.axis_size("store") // row_count
    part_rows = flat_rows.reshape(block_count, row_count, feature_total)
    products = jnp.einsum(
        "nrf,nfk->nrk", part_rows, selected_first_factor, preferred_element_type=jnp.float32
    )
    partial_sums = lax.psum_scatter(
        products.reshape(row_count * lax.axis_size("store"), -1),
        "store",
        scatter_dimension=0,
        tiled=True,
    )
    full_sums = lax.psum(partial_sums, "tp")
    rank_projection = full_sums.astype(jnp.bfloat16)
    rank_length = adapter_second_factor.shape[2]
    key_value_width = adapter_second_factor.shape[3]
    own_adapter = request_adapter[0]
    local_block_rows = lax.all_gather(adapter_second_factor, "store", axis=0, tiled=True)
    inside_mask = (own_adapter >= 0) & (own_adapter < local_block_rows.shape[0])
    candidate_adapter = lax.dynamic_index_in_dim(
        local_block_rows, jnp.clip(own_adapter, 0, local_block_rows.shape[0] - 1), 0, keepdims=False
    )
    picked_adapter = jnp.where(
        inside_mask, candidate_adapter, jnp.zeros(adapter_second_factor.shape[1:], jnp.bfloat16)
    )
    adapter_update = jnp.einsum(
        "zlo,lom->zlm",
        rank_projection.reshape(row_count, 2, rank_length),
        picked_adapter,
        preferred_element_type=jnp.float32,
    )
    positions = jnp.arange(row_count)
    live_rows = positions < block_live_length[0]
    updated_key_value = plain_key_value.astype(jnp.float32) + adapter_update
    rotated = rotate_keys(
        updated_key_value[:, 0].reshape(row_count, key_value_width // HEAD_WIDTH, HEAD_WIDTH),
        context_length[0] + positions,
    ).reshape(row_count, key_value_width)
    stacked = jnp.stack([rotated, updated_key_value[:, 1]], axis=1)
    new_kv = jnp.where(live_rows[:, None, None], stacked, 0.0).astype(jnp.bfloat16)
    attention_out = attend_block(queries, cached_key_value, new_kv, live_rows, context_length[0])
    return (new_kv, attention_out)


def solution(mesh):
    in_specs = (
        P(("store", "req"), None),
        P(("store", "req"), "tp"),
        P(("store", "req"), None, "tp"),
        P(("store", "req"), None, None, "tp"),
        P(None, ("store", "tp"), None),
        P("store", None, None, "tp"),
        P(("store", "req")),
        P(("store", "req")),
        P(("store", "req")),
    )
    out_specs = (P(("store", "req"), None, "tp"), P(("store", "req"), "tp"))
    return jax.shard_map(shards, mesh=mesh, in_specs=in_specs, out_specs=out_specs, check_vma=False)
```

profile of v0, /device:TPU:1, one launch (start us, length us, event | category | flops | bytes accessed | tf_op | source)
XLA Modules:
  0.0 440.0 jit_solution(4348678404006551978)
XLA Ops:
  8.0 0.6 broadcast_in_dim.93
  8.6 12.0 %all-to-all-start.1 = ((s32[1,32,1]{2,0,1:T(1,128)}), s32[1,32,1]{2,0,1:T(1,128)S(1)}, u32[]{:S(2)}, u32[]{:S(2)}) async-start(s32[1,32,1]{2,0,1:T(1,128)} %broadcast_in_dim.93), calls=%async_computation.1 | async-start | bytes 32768 | tf_op jit(solution)/shard_map/all_to_all | solution.py:96
  20.6 4.4 %reshape.198 = bf16[128,32,2,128]{3,2,1,0:T(2,128)(2,1)} reshape(bf16[128,8192]{1,0:T(8,128)(2,1)} %param.11) | data formatting | bytes 4194304 | tf_op jit(solution)/shard_map/reshape | solution.py:91
  25.1 4.0 constant_dynamic-slice_fusion
  29.1 2.2 copy.67
  31.3 9.4 %all-to-all-start = ((bf16[128,32,128]{2,0,1:T(8,128)(2,1)}), bf16[128,32,128]{2,0,1:T(8,128)(2,1)}, u32[]{:S(2)}, u32[]{:S(2)}) async-start(bf16[128,32,128]{2,0,1:T(8,128)(2,1)} %bitcast.99), calls=%async_computation | async-start | bytes 2097152 | tf_op jit(solution)/shard_map/all_to_all | solution.py:95
  40.7 0.7 reduce.1
  41.4 0.7 gather_fusion
  42.2 23.1 %all-to-all-done = bf16[128,32,128]{2,0,1:T(8,128)(2,1)} async-done(((bf16[128,32,128]{2,0,1:T(8,128)(2,1)}), bf16[128,32,128]{2,0,1:T(8,128)(2,1)}, u32[]{:S(2)}, u32[]{:S(2)}) %all-to-all-start) | async-done | bytes 1048608 | tf_op jit(solution)/shard_map/all_to_all | solution.py:95
  65.3 3.1 fusion.36
  68.5 0.7 all-gather.2.cloned.1.call-update
  69.2 1.2 copy.48
  71.6 4.4 %fusion.52 = (bf16[1,1,2048,512]{3,2,1,0:T(8,128)(2,1)}, bf16[1,1,2048,512]{3,2,1,0:T(8,128)(2,1)}) fusion(bf16[1,2,2048,512]{3,2,1,0:T(8,128)(2,1)} %param.14), kind=kLoop, calls=%fused_computation.78 | loop fusion | bytes 8388608 | tf_op jit(solution)/shard_map/slice | solution.py:37
  76.1 4.0 copy.51
  80.0 3.9 copy.64
  84.0 1.6 copy.53
  85.8 194.5 %reduce-scatter.2.cloned.1.call-done = f32[128,128]{1,0:T(8,128)} async-done(((f32[4096,128]{1,0:T(8,128)}), f32[128,128]{1,0:T(8,128)}) %reduce-scatter.2.cloned.1.call-update) | async-done | bytes 65552 | tf_op jit(solution)/shard_map/reduce_scatter | solution.py:106
  280.4 10.1 %psum.7 = bf16[128,128]{1,0:T(8,128)(2,1)S(1)} all-reduce(f32[128,128]{1,0:T(8,128)} %reduce-scatter.2.cloned.1.call-done), channel_id=1, replica_groups=mesh['store'=32,'req'=4,'tp'=2] {'tp'}, use_global_device_ids=true, to_apply=%region_1.2 | all-reduce | flops 16384 | bytes 98304 | tf_op jit(solution)/shard_map/psum | solution.py:112
  290.6 94.3 %all-gather.2.cloned.1.call-done = bf16[64,2,64,512]{3,2,1,0:T(8,128)(2,1)} async-done(((bf16[2,2,64,512]{3,2,1,0:T(8,128)(2,1)}), bf16[64,2,64,512]{3,2,1,0:T(8,128)(2,1)}) %all-gather.2.cloned.1.call-update) | async-done | bytes 8388624 | tf_op jit(solution)/shard_map/all_gather | solution.py:117
  384.9 1.2 fusion.35
  386.3 0.7 fusion.53
  386.9 0.9 copy.58
  387.9 42.5 %while.11 = (s32[]{:T(128)}, bf16[4,128,8,128]{1,3,2,0:T(8,128)(2,1)}, bf16[4,2048,128]{1,2,0:T(8,128)(2,1)}, bf16[4,2048,128]{1,2,0:T(8,128)(2,1)}, bf16[4,128,...) while((s32[]{:T(128)}, ...), condition=%wide.region_7.8_spmd.clone, body=%wide.region_2.7_spmd.clone.sunk | while | flops 1167228928 | bytes 30060264 | solution.py:70
  387.9 0.7 compare_reduce_fusion.2
  388.6 2.5 bitcast_reduce_fusion.2
  391.2 0.2 fusion.66
  391.6 1.8 fusion.67
  393.4 3.4 fusion.69
  396.8 1.7 fusion.70
  398.6 0.7 compare_reduce_fusion.2
  399.2 2.5 bitcast_reduce_fusion.2
  401.8 0.2 fusion.66
  402.2 1.8 fusion.67
  404.1 3.4 fusion.69
  407.5 1.7 fusion.70
  409.2 0.7 compare_reduce_fusion.2
  409.9 2.5 bitcast_reduce_fusion.2
  412.8 1.8 fusion.67
  414.7 3.4 fusion.69
  418.1 1.7 fusion.70
  419.8 0.7 compare_reduce_fusion.2
  420.5 2.5 bitcast_reduce_fusion.2
  423.1 0.2 fusion.66
  423.4 1.8 fusion.67
  425.3 3.4 fusion.69
  428.7 1.7 fusion.70
  430.4 1.5 copy.61
  431.9 1.2 select_convert_fusion
  (38 shorter events, 1.7 us)
Async XLA Ops:
  7.2 34.2 %copy-start = (bf16[64,128,128]{2,1,0:T(8,128)(2,1)S(1)}, bf16[64,128,128]{2,1,0:T(8,128)(2,1)}, u32[]{:S(2)}) copy-start(bf16[64,128,128]{2,1,0:T(8,128)(2,1)} %param.15) | copy-start | bytes 6291460
  8.6 22.7 %all-to-all-start.1 = ((s32[1,32,1]{2,0,1:T(1,128)}), s32[1,32,1]{2,0,1:T(1,128)S(1)}, u32[]{:S(2)}, u32[]{:S(2)}) async-start(s32[1,32,1]{2,0,1:T(1,128)} %broadcast_in_dim.93), calls=%async_computation.1 | async-start | bytes 32768 | tf_op jit(solution)/shard_map/all_to_all | solution.py:96
  31.3 34.0 %all-to-all-start = ((bf16[128,32,128]{2,0,1:T(8,128)(2,1)}), bf16[128,32,128]{2,0,1:T(8,128)(2,1)}, u32[]{:S(2)}, u32[]{:S(2)}) async-start(bf16[128,32,128]{2,0,1:T(8,128)(2,1)} %bitcast.99), calls=%async_computation | async-start | bytes 2097152 | tf_op jit(solution)/shard_map/all_to_all | solution.py:95
  40.7 239.7 %reduce-scatter.2.cloned.1.call-start = ((), (), s32[]{:S(2)}) async-start(), calls=%async_computation.4 | async-start | bytes 2162688 | tf_op jit(solution)/shard_map/reduce_scatter | solution.py:106
  68.4 316.5 %all-gather.2.cloned.1.call-start = ((), (), s32[]{:S(2)}) async-start(), calls=%async_computation.3 | async-start | bytes 8650752 | tf_op jit(solution)/shard_map/all_gather | solution.py:117
Sparse Core Ops, SparseCore 0:
  68.5 211.7 reduce-scatter.1
  283.3 101.5 all-gather.1
where the time goes:
time: 441 us; the launch traced here: 440 us
  waiting for transfers between devices  313 us (71%)
  matrix products  35.7 us (8%)
  local copies, waits for them, and re-layouts  30.4 us (7%)
  starting transfers between devices  21.5 us (5%)
  between operations  16.3 us (4%)
  other arithmetic  13.1 us (3%)
  blocking collectives  10.1 us (2%)
    reduce_scatter x1, waiting for transfers between devices, shards(): lax.psum_scatter(products.reshape(row_count * lax.axis_size('store'), -1)...  195 us
    all_gather x1, waiting for transfers between devices, shards(): lax.all_gather(adapter_second_factor, 'store', axis=0, tiled=True)  94.3 us
    all_to_all x1, waiting for transfers between devices, shards(): lax.all_to_all(own_half, 'store', split_axis=1, concat_axis=0, tiled=True)  23.1 us
    dot_general x4, matrix products, one_head(): jnp.einsum('gij,jd->igd', weight_old, values_old, preferred_element_type=...  13.5 us
    all_to_all x1, starting transfers between devices, shards(): lax.all_to_all(id_slots, 'store', split_axis=1, concat_axis=0, tiled=True)  12 us
    psum x1, blocking collectives, shards(): full_sums = lax.psum(partial_sums, 'tp')  10.1 us
    dot_general x4, matrix products, one_head(): jnp.einsum('igd,jd->gij', query_rows, keys_old, preferred_element_type=jn...  10 us
    unnamed x7, local copies, waits for them, and re-layouts  9.78 us
  transfers between devices with their start and end apart: 4, of which 3 were waited for; matrix products, arithmetic and copies ran while one was open for 6% of the time, Pallas kernels for 0%

commit v1 on v0

v1 whole, which is shorter than its diff:
```python
import functools
import math

import jax
import jax.numpy as jnp
from jax import lax
from jax.experimental import pallas as pl
from jax.experimental.pallas import tpu as pltpu
from jax.sharding import PartitionSpec as P

HEAD = 128
ROWS = 128
RANK = 64
NY, NZ, NX = 4, 8, 4
PLANE = NY * NZ
GROUP = 8
KV_HEADS = 4
CTX = 2048
TILE = 512
SCALE2 = math.log2(math.e) / math.sqrt(HEAD)
LOWEST = -1e30
MESH = pl.DeviceIdType.MESH

OFFSETS = sorted(
    [(dy, dz) for dy in range(NY) for dz in range(NZ) if (dy, dz) != (0, 0)],
    key=lambda o: -(2 * min(o[1], NZ - o[1]) + min(o[0], NY - o[0])),
)


def slot(dy, dz):
    return (dy % NY) * NZ + dz % NZ


def kernel(
    adapter_ref, live_ref, ctx_ref, tokens, queries, plain, cached, first, second,
    new_out, attn_out,
    tok_v, q_v, plain_v, kv_v, first_v, send_a, recv_a, gath, send2, recv2, send3, recv3,
    part, part_in, key_buf, val_buf, acc, top, cos_v, sin_v, new_v, out_v, ids, xids,
    lsem, kvsem, osem, id_s, id_r, xid_s, xid_r, a_s, a_r, b1_s, b1_r, b2_s, b2_r, b3_s, b3_r, p_s, p_r,
):
    store, req, core = lax.axis_index("store"), lax.axis_index("req"), lax.axis_index("tp")
    y, z = store // NZ, lax.rem(store, NZ)

    def plane(dy, dz):
        return {"store": lax.rem(y + dy % NY, NY) * NZ + lax.rem(z + dz % NZ, NZ)}

    def across(dx):
        return {"req": lax.rem(req + dx % NX, NX)}

    sibling = {"tp": 1 - core}

    def remote(src, dst, s, r, dev):
        return pltpu.make_async_remote_copy(
            src_ref=src, dst_ref=dst, send_sem=s, recv_sem=r, device_id=dev, device_id_type=MESH
        )

    bar = pltpu.get_barrier_semaphore()
    peers = [plane(*o) for o in OFFSETS] + [across(dx) for dx in range(1, NX)] + [sibling]
    for dev in peers:
        pl.semaphore_signal(bar, inc=1, device_id=dev, device_id_type=MESH)

    def head_cols(h):
        return pl.ds(h * HEAD, HEAD)

    load_q = pltpu.make_async_copy(queries, q_v, lsem.at[0])
    load_q.start()
    load_kv = []
    for h in range(KV_HEADS):
        c = pltpu.make_async_copy(
            cached.at[0, :, :, head_cols(h)], kv_v.at[:, :, head_cols(h)], kvsem.at[h]
        )
        c.start()
        load_kv.append(c)
    load_b = pltpu.make_async_copy(
        second.at[:, :, pl.ds(pl.multiple_of(req * 16, 16), 16), :], gath.at[0], lsem.at[1]
    )
    load_b.start()
    load_a = pltpu.make_async_copy(first, first_v, lsem.at[2])
    load_a.start()
    load_p = pltpu.make_async_copy(plain, plain_v, lsem.at[3])
    load_p.start()
    load_t = pltpu.make_async_copy(tokens, tok_v, lsem.at[4])
    load_t.start()

    ctx = ctx_ref[0]
    live = live_ref[0]
    ids[0, 0] = adapter_ref[0]

    def attend(h):
        load_kv[h].wait()
        alive = lax.broadcasted_iota(jnp.int32, (CTX, HEAD), 0) < ctx
        k = kv_v[0, :, head_cols(h)]
        v = kv_v[1, :, head_cols(h)]
        key_buf[...] = jnp.where(alive, k, jnp.broadcast_to(k[0:1, :], k.shape))
        val_buf[:, 0:HEAD] = jnp.where(alive, v, jnp.zeros_like(v))
        val_buf[:, HEAD:] = jnp.where(alive, jnp.ones_like(v), jnp.zeros_like(v))
        per = TILE // ROWS
        for u in range(GROUP // per):
            g = h * GROUP + u * per
            q = jnp.concatenate([q_v[:, head_cols(g + i)] for i in range(per)], axis=0)
            s = lax.dot_general(
                q, key_buf[...], (((1,), (1,)), ((), ())), preferred_element_type=jnp.float32
            )
            m = jnp.max(s, axis=1, keepdims=True)
            p = jnp.exp2(s * SCALE2 - m * SCALE2).astype(jnp.bfloat16)
            r = pl.ds(g * ROWS, TILE)
            acc[r, :] = jnp.dot(p, val_buf[...], preferred_element_type=jnp.float32)
            m = jnp.where(ctx > 0, m, LOWEST)
            top[r, :] = jnp.broadcast_to(m, (TILE, HEAD))

    load_q.wait()
    attend(0)

    lane = lax.broadcasted_iota(jnp.int32, (ROWS, HEAD), 1)
    row = lax.broadcasted_iota(jnp.int32, (ROWS, HEAD), 0)
    index = jnp.where(lane < HEAD // 2, lane, lane - HEAD // 2).astype(jnp.float32)
    frequency = jnp.exp(index * (-2.0 / HEAD * math.log(10000.0)))
    angle = (ctx + row).astype(jnp.float32) * frequency
    cos_v[...] = jnp.cos(angle)
    sine = jnp.sin(angle)
    sin_v[...] = jnp.where(lane < HEAD // 2, -sine, sine)

    pl.semaphore_wait(bar, len(peers))

    id_copies = []
    for dy, dz in OFFSETS:
        k = slot(dy, dz)
        c = remote(adapter_ref, ids.at[k], id_s.at[k], id_r.at[k], plane(dy, dz))
        c.start()
        id_copies.append(c)
    load_b.wait()
    b1 = []
    for dz in sorted(range(1, NZ), key=lambda d: -min(d, NZ - d)):
        c = remote(gath.at[0], gath.at[dz], b1_s.at[dz], b1_r.at[dz], plane(0, dz))
        c.start()
        b1.append(c)

    attend(1)

    for c in id_copies:
        c.wait()
    xid_copies = []
    for dx in range(1, NX):
        c = remote(ids, xids.at[dx], xid_s.at[dx], xid_r.at[dx], across(dx))
        c.start()
        xid_copies.append(c)
    load_a.wait()
    a_copies = {}
    for dy, dz in OFFSETS:
        k = slot(dy, dz)
        send_a[k] = first_v[ids[slot(-dy, -dz), 0]]
        c = remote(send_a.at[k], recv_a.at[k], a_s.at[k], a_r.at[k], plane(dy, dz))
        c.start()
        a_copies[k] = c
    recv_a[0] = first_v[ids[0, 0]]

    attend(2)

    for c in xid_copies:
        c.wait()
    for c in b1:
        c.wait()

    def request_id(dx, k):
        return ids[k, 0] if dx == 0 else xids[dx, k, 0]

    b2 = []
    for dy in (2, 1, 3, 0):
        for dx in range(NX):
            a = request_id(dx, slot(-dy, 0))
            from_z = jnp.bitwise_and(jnp.right_shift(a, 1), NZ - 1)
            there = jnp.bitwise_and(z - from_z + NZ, NZ - 1)
            piece = gath[there, jnp.bitwise_and(a, 1)]
            if dy == 0:
                recv2[0, dx] = piece
            else:
                send2[dy, dx] = piece
        if dy:
            c = remote(send2.at[dy], recv2.at[dy], b2_s.at[dy], b2_r.at[dy], plane(dy, 0))
            c.start()
            b2.append(c)

    attend(3)

    for c in b2:
        c.wait()
    b3 = []
    for dx in (2, 1, 3, 0):
        a = request_id(dx, 0)
        from_y = jnp.bitwise_and(jnp.right_shift(a, 4), NY - 1)
        there = jnp.bitwise_and(y - from_y + NY, NY - 1)
        piece = recv2[there, dx]
        if dx == 0:
            recv3[0] = piece
        else:
            send3[dx] = piece
            c = remote(send3.at[dx], recv3.at[dx], b3_s.at[dx], b3_r.at[dx], across(-dx))
            c.start()
            b3.append(c)

    load_t.wait()

    def token_cols(dy, dz):
        owner = lax.rem(y - dy + NY, NY) * NZ + lax.rem(z - dz + NZ, NZ)
        return tok_v[:, pl.ds(pl.multiple_of((owner * 2 + core) * 128, 128), 128)]

    order = sorted([(dy, dz) for dy in range(NY) for dz in range(NZ)],
                   key=lambda o: (2 * min(o[1], NZ - o[1]) + min(o[0], NY - o[0])))
    total = jnp.zeros((ROWS, 2 * RANK), jnp.float32)
    for lo in range(0, PLANE, 4):
        some = order[lo:lo + 4]
        for o in some:
            if o != (0, 0):
                a_copies[slot(*o)].wait()
        left = jnp.concatenate([token_cols(*o) for o in some], axis=1)
        right = jnp.concatenate([recv_a[slot(*o)] for o in some], axis=0)
        total = total + jnp.dot(left, right, preferred_element_type=jnp.float32)
    part[...] = total
    swap = remote(part, part_in, p_s, p_r, sibling)
    swap.start()
    for c in b3:
        c.wait()
    load_p.wait()
    swap.wait()
    rank = (part[...] + part_in[...]).astype(jnp.bfloat16)

    alive = lax.broadcasted_iota(jnp.int32, (ROWS, HEAD), 0) < live
    for j in range(2):
        base = plain_v[:, j, :].astype(jnp.float32)
        whole = jnp.concatenate([recv3[jnp.bitwise_and(x - req + NX, NX - 1), j] for x in range(NX)], axis=0)
        delta = jnp.dot(rank[:, j * RANK:(j + 1) * RANK], whole, preferred_element_type=jnp.float32)
        fresh = base + delta
        for h in range(KV_HEADS):
            one = fresh[:, h * HEAD:(h + 1) * HEAD]
            if j == 0:
                one = one * cos_v[...] + pltpu.roll(one, HEAD // 2, 1) * sin_v[...]
            new_v[j, :, head_cols(h)] = jnp.where(alive, one, 0.0).astype(jnp.bfloat16)
    put_new = pltpu.make_async_copy(new_v, new_out, osem.at[KV_HEADS])
    put_new.start()

    column = lax.broadcasted_iota(jnp.int32, (ROWS, HEAD), 1)
    allowed = (column <= row) & (column < live)
    puts = []
    for h in range(KV_HEADS):
        kn = new_v[0, :, head_cols(h)]
        vn = jnp.concatenate([new_v[1, :, head_cols(h)], jnp.ones((ROWS, HEAD), jnp.bfloat16)], axis=1)
        q = jnp.concatenate([q_v[:, head_cols(h * GROUP + i)] for i in range(GROUP)], axis=0)
        s = lax.dot_general(q, kn, (((1,), (1,)), ((), ())), preferred_element_type=jnp.float32)
        s = jnp.where(allowed[None], s.reshape(GROUP, ROWS, HEAD), LOWEST).reshape(GROUP * ROWS, HEAD)
        r = pl.ds(h * GROUP * ROWS, GROUP * ROWS)
        old = top[r, :]
        m = jnp.maximum(jnp.max(s, axis=1, keepdims=True), old)
        p = jnp.exp2((s - m) * SCALE2).astype(jnp.bfloat16)
        o = jnp.dot(p, vn, preferred_element_type=jnp.float32)
        alpha = jnp.exp2((old - m) * SCALE2)
        top_part = acc[r, 0:HEAD] * alpha + o[:, 0:HEAD]
        bottom = acc[r, HEAD:] * alpha + o[:, HEAD:]
        res = top_part / bottom
        for g in range(GROUP):
            one = jnp.where(alive, res[g * ROWS:(g + 1) * ROWS, :], 0.0)
            out_v[:, head_cols(h * GROUP + g)] = one.astype(jnp.bfloat16)
        cols = pl.ds(h * GROUP * HEAD, GROUP * HEAD)
        c = pltpu.make_async_copy(out_v.at[:, cols], attn_out.at[:, cols], osem.at[h])
        c.start()
        puts.append(c)
    for c in puts:
        c.wait()
    put_new.wait()


def shards(tokens, queries, plain, cached, first, second, adapter, live, ctx):
    width = plain.shape[2]
    bf16, f32 = jnp.bfloat16, jnp.float32
    dma = pltpu.SemaphoreType.DMA
    smem = pl.BlockSpec(memory_space=pltpu.SMEM)
    hbm = pl.BlockSpec(memory_space=pl.ANY)
    heads = KV_HEADS * GROUP
    new, attn = pl.pallas_call(
        kernel,
        out_shape=(
            jax.ShapeDtypeStruct((2, ROWS, width), bf16),
            jax.ShapeDtypeStruct(queries.shape, bf16),
        ),
        in_specs=[smem] * 3 + [hbm] * 6,
        out_specs=(hbm, hbm),
        scratch_shapes=[
            pltpu.VMEM(tokens.shape, bf16),
            pltpu.VMEM(queries.shape, bf16),
            pltpu.VMEM(plain.shape, bf16),
            pltpu.VMEM((2, CTX, width), bf16),
            pltpu.VMEM(first.shape, bf16),
            pltpu.VMEM((PLANE, 128, 2 * RANK), bf16),
            pltpu.VMEM((PLANE, 128, 2 * RANK), bf16),
            pltpu.VMEM((NZ, 2, 2, 16, width), bf16),
            pltpu.VMEM((NY, NX, 2, 16, width), bf16),
            pltpu.VMEM((NY, NX, 2, 16, width), bf16),
            pltpu.VMEM((NX, 2, 16, width), bf16),
            pltpu.VMEM((NX, 2, 16, width), bf16),
            pltpu.VMEM((ROWS, 2 * RANK), f32),
            pltpu.VMEM((ROWS, 2 * RANK), f32),
            pltpu.VMEM((CTX, HEAD), bf16),
            pltpu.VMEM((CTX, 2 * HEAD), bf16),
            pltpu.VMEM((heads * ROWS, 2 * HEAD), f32),
            pltpu.VMEM((heads * ROWS, HEAD), f32),
            pltpu.VMEM((ROWS, HEAD), f32),
            pltpu.VMEM((ROWS, HEAD), f32),
            pltpu.VMEM((2, ROWS, width), bf16),
            pltpu.VMEM(queries.shape, bf16),
            pltpu.SMEM((PLANE, 1), jnp.int32),
            pltpu.SMEM((NX, PLANE, 1), jnp.int32),
            dma((5,)), dma((KV_HEADS,)), dma((KV_HEADS + 1,)),
            dma((PLANE,)), dma((PLANE,)), dma((NX,)), dma((NX,)),
            dma((PLANE,)), dma((PLANE,)), dma((NZ,)), dma((NZ,)),
            dma((NY,)), dma((NY,)), dma((NX,)), dma((NX,)), dma, dma,
        ],
        compiler_params=pltpu.CompilerParams(
            collective_id=0, has_side_effects=True, vmem_limit_bytes=58 << 20
        ),
    )(adapter, live, ctx, tokens, queries, plain, cached, first, second)
    return jnp.transpose(new, (1, 0, 2)), attn


def solution(mesh):
    in_specs = (
        P(("store", "req"), None),
        P(("store", "req"), "tp"),
        P(("store", "req"), None, "tp"),
        P(("store", "req"), None, None, "tp"),
        P(None, ("store", "tp"), None),
        P("store", None, None, "tp"),
        P(("store", "req")),
        P(("store", "req")),
        P(("store", "req")),
    )
    out_specs = (P(("store", "req"), None, "tp"), P(("store", "req"), "tp"))
    return jax.shard_map(shards, mesh=mesh, in_specs=in_specs, out_specs=out_specs, check_vma=False)
```

time: 441 us -> 63.5 us (0.14)
  waiting for transfers between devices: 313 us -> 0 us
  Pallas kernels: 0 us -> 56.6 us
  matrix products: 35.7 us -> 0 us
  local copies, waits for them, and re-layouts: 30.4 us -> 4.21 us
  starting transfers between devices: 21.5 us -> 0 us
  between operations: 16.3 us -> 2.58 us
  other arithmetic: 13.1 us -> 0 us
  blocking collectives: 10.1 us -> 0 us
    reduce_scatter x1 -> x0, waiting for transfers between devices: 195 us -> none  [shards(): lax.psum_scatter(products.reshape(row_count * lax.axis_size('store'), -1)...]
    all_gather x1 -> x0, waiting for transfers between devices: 94.3 us -> none  [shards(): lax.all_gather(adapter_second_factor, 'store', axis=0, tiled=True)]
    pallas_call x0 -> x1, Pallas kernels: none -> 56.6 us  [shards(): pl.pallas_call(kernel, out_shape=(jax.ShapeDtypeStruct((2, ROWS, width),...]
    dot_general x18 -> x0, matrix products: 35.7 us -> none  [the longest x4 13.5 us: one_head(): jnp.einsum('gij,jd->igd', weight_old, values_old, preferred_element_type=...]
    all_to_all x2 -> x0, waiting for transfers between devices: 23.1 us -> none  [the longest x1 23.1 us: shards(): lax.all_to_all(own_half, 'store', split_axis=1, concat_axis=0, tiled=True)]
    all_to_all x2 -> x0, starting transfers between devices: 21.4 us -> none  [the longest x1 12 us: shards(): lax.all_to_all(id_slots, 'store', split_axis=1, concat_axis=0, tiled=True)]
    psum x1 -> x0, blocking collectives: 10.1 us -> none  [shards(): full_sums = lax.psum(partial_sums, 'tp')]
    slice x5 -> x0, local copies, waits for them, and re-layouts: 9.08 us -> none  [the longest x1 4.42 us: attend_block(): cached_key_value[0, 0].reshape(context, kv_heads, HEAD_WIDTH)]
  transfers between devices with their start and end apart: 4 -> 0, of which waited for: 3 -> 0; matrix products, arithmetic and copies ran while one was open for 6% -> 0% of each run, Pallas kernels for 0% -> 0%
where the time goes in v1:
time: 63.5 us; the launch traced here: 63.4 us
  Pallas kernels  56.6 us (89%)
  local copies, waits for them, and re-layouts  4.21 us (7%)
  between operations  2.58 us (4%)
    pallas_call x1, Pallas kernels, shards(): pl.pallas_call(kernel, out_shape=(jax.ShapeDtypeStruct((2, ROWS, width),...  56.6 us
    unnamed x2, local copies, waits for them, and re-layouts  4.21 us

profile of v1, /device:TPU:1, one launch (start us, length us, event | category | flops | bytes accessed | tf_op | source)
XLA Modules:
  0.0 63.4 jit_solution(13377023650768381958)
XLA Ops:
  2.6 56.6 %shard_map.104 = (bf16[2,128,512]{2,1,0:T(8,128)(2,1)}, bf16[128,4096]{1,0:T(8,128)(2,1)}) custom-call(s32[1]{0:T(128)S(6)} %copy.13.adapter_ref, s32[1]{0:T(128)S(6)} %copy.14.live_ref, s32[1]{0:T(128)S(6)} %copy.15.ctx_ref, bf16[128,8192]{1,0:T(8,128)(2,1)} %tokens.1, bf16[128,4096]{1,0:T(8,128)(2,1)} %queries.1, bf16[128,2,512]{2,1,0:T(2,128)(2,1)} %plain.1, ...), custom_call_target="tpu_custom_call" | custom-call | tf_op jit(solution)/shard_map/pallas_call | solution.py:278
  59.1 1.9 %copy.11 = bf16[128,2,512]{2,1,0:T(2,128)(2,1)} copy(bf16[128,2,512]{2,0,1:T(8,128)(2,1)} %bitcast.1) | data formatting | bytes 524288
  61.1 2.3 %copy.16 = bf16[128,4096]{1,0:T(8,128)(2,1)} copy(bf16[128,4096]{1,0:T(8,128)(2,1)} %get-tuple-element.11) | data formatting | bytes 2097152

commit v2 on v1

v2 whole, which is shorter than its diff:
```python
import functools
import math

import jax
import jax.numpy as jnp
from jax import lax
from jax.experimental import pallas as pl
from jax.experimental.pallas import tpu as pltpu
from jax.sharding import PartitionSpec as P

HEAD = 128
ROWS = 128
RANK = 64
NY, NZ, NX = 4, 8, 4
PLANE = NY * NZ
GROUP = 8
KV_HEADS = 4
CTX = 2048
TILE = 512
SCALE2 = math.log2(math.e) / math.sqrt(HEAD)
LOWEST = -1e30
FAR_X = (2, 1, 3)
FAR_Y = (2, 1, 3)
FAR_Z = (4, 3, 5, 2, 6, 1, 7)
REST = (1, 7, 3, 5, 4, 0)
MESH = pl.DeviceIdType.MESH

def slot(dy, dz):
    return (dy % NY) * NZ + dz % NZ


def head_cols(h):
    return pl.ds(h * HEAD, HEAD)


def kernel(
    adapter_ref, live_ref, ctx_ref, tokens, queries, plain, cached, first, second,
    new_out, attn_out,
    tok_v, q_v, plain_v, base_v, kv_v, first_v, send_a, recv_a, gath, send2, recv2, send3, recv3,
    part, part_in, key_buf, val_buf, acc, top, angle_v, new_v, out_v, col, ids, xids,
    lsem, kvsem, osem, idy_s, idy_r, idz_s, idz_r, xid_s, xid_r, a_s, a_r,
    b1_s, b1_r, b2_s, b2_r, b3_s, b3_r, p_s, p_r,
):
    store, req, core = lax.axis_index("store"), lax.axis_index("req"), lax.axis_index("tp")
    y, z = store // NZ, lax.rem(store, NZ)

    def plane(dy, dz):
        return {"store": lax.rem(y + dy % NY, NY) * NZ + lax.rem(z + dz % NZ, NZ)}

    def across(dx):
        return {"req": lax.rem(req + dx % NX, NX)}

    sibling = {"tp": 1 - core}
    sends = []

    def remote(src, dst, s, r, dev):
        c = pltpu.make_async_remote_copy(
            src_ref=src, dst_ref=dst, send_sem=s, recv_sem=r, device_id=dev, device_id_type=MESH
        )
        c.start()
        sends.append(c)
        return c

    bar = pltpu.get_barrier_semaphore()
    peers = [plane(0, dz) for dz in FAR_Z] + [plane(dy, 0) for dy in FAR_Y]
    peers += [across(dx) for dx in FAR_X] + [sibling]
    for dev in peers:
        pl.semaphore_signal(bar, inc=1, device_id=dev, device_id_type=MESH)

    def load(src, dst, i):
        c = pltpu.make_async_copy(src, dst, lsem.at[i])
        c.start()
        return c

    load_q = load(queries, q_v, 0)
    load_kv = []
    for h in range(KV_HEADS):
        c = pltpu.make_async_copy(
            cached.at[0, :, :, head_cols(h)], kv_v.at[:, :, head_cols(h)], kvsem.at[h]
        )
        c.start()
        load_kv.append(c)
        if h == 0:
            load_b = load(second.at[:, :, pl.ds(pl.multiple_of(req * 16, 16), 16), :], gath.at[0], 1)
            load_p = load(plain, plain_v, 3)
            load_a = load(first, first_v, 2)
    load_t = load(tokens, tok_v, 4)

    ctx = ctx_ref[0]
    live = live_ref[0]
    col[0, 0] = adapter_ref[0]

    def attend(h, u):
        if u == 0:
            prepare(h)
        per = TILE // ROWS
        g = h * GROUP + u * per
        q = jnp.concatenate([q_v[:, head_cols(g + i)] for i in range(per)], axis=0)
        s = lax.dot_general(
            q, key_buf[...], (((1,), (1,)), ((), ())), preferred_element_type=jnp.float32
        )
        m = jnp.max(s, axis=1, keepdims=True) * SCALE2
        p = jnp.exp2(s * SCALE2 - m).astype(jnp.bfloat16)
        r = pl.ds(g * ROWS, TILE)
        acc[r, :] = jnp.dot(p, val_buf[...], preferred_element_type=jnp.float32)
        m = jnp.where(ctx > 0, m, LOWEST)
        top[r, :] = jnp.broadcast_to(m, (TILE, HEAD))

    def prepare(h):
        load_kv[h].wait()
        alive = lax.broadcasted_iota(jnp.int32, (CTX, HEAD), 0) < ctx
        k = kv_v[0, :, head_cols(h)]
        v = kv_v[1, :, head_cols(h)]
        key_buf[...] = jnp.where(alive, k, jnp.broadcast_to(k[0:1, :], k.shape))
        val_buf[:, 0:HEAD] = jnp.where(alive, v, jnp.zeros_like(v))
        val_buf[:, HEAD:] = jnp.where(alive, jnp.ones_like(v), jnp.zeros_like(v))

    load_q.wait()
    attend(0, 0)
    attend(0, 1)

    lane = lax.broadcasted_iota(jnp.int32, (ROWS, HEAD), 1)
    row = lax.broadcasted_iota(jnp.int32, (ROWS, HEAD), 0)
    index = jnp.where(lane < HEAD // 2, lane, lane - HEAD // 2).astype(jnp.float32)
    frequency = jnp.exp(index * (-2.0 / HEAD * math.log(10000.0)))
    angle = (ctx + row).astype(jnp.float32) * frequency
    angle_v[0] = jnp.cos(angle)
    sine = jnp.sin(angle)
    angle_v[1] = jnp.where(lane < HEAD // 2, -sine, sine)
    load_p.wait()
    for j in range(2):
        base_v[j] = plain_v[:, j, :]

    pl.semaphore_wait(bar, len(peers))

    id_y = {dy: remote(adapter_ref, col.at[dy], idy_s.at[dy], idy_r.at[dy], plane(dy, 0)) for dy in FAR_Y}
    load_b.wait()
    near = {}

    def pass_near(dz):
        near[dz] = remote(gath.at[0], gath.at[dz], b1_s.at[dz], b1_r.at[dz], plane(0, dz))

    def pass_on():
        for dz in (2, 6):
            near[dz].wait_recv()
        near[3] = remote(gath.at[2], gath.at[3], b1_s.at[3], b1_r.at[3], plane(0, 1))
        near[5] = remote(gath.at[6], gath.at[5], b1_s.at[5], b1_r.at[5], plane(0, -1))
        near[4] = remote(gath.at[2, 0], gath.at[4, 0], b1_s.at[4], b1_r.at[4], plane(0, 2))
        near[0] = remote(gath.at[6, 1], gath.at[4, 1], b1_s.at[0], b1_r.at[0], plane(0, -2))

    blocks = {}

    def send_block(dy, dz):
        k = slot(dy, dz)
        send_a[k] = first_v[col[-dy % NY, 0] if dz == 0 else ids[-dz % NZ, -dy % NY, 0]]
        blocks[k] = remote(send_a.at[k], recv_a.at[k], a_s.at[k], a_r.at[k], plane(dy, dz))

    def send_group(dz):
        if dz:
            id_z[-dz % NZ].wait_recv()
        else:
            recv_a[0] = first_v[col[0, 0]]
        for dy in FAR_Y + ((0,) if dz else ()):
            send_block(dy, dz)

    def request_id(dx, dy):
        return col[dy % NY, 0] if dx == 0 else xids[dx, dy % NY, 0]

    b2 = []

    def along_y():
        for c in id_x:
            c.wait_recv()
        for dz in REST:
            near[dz].wait_recv()
        for dy in FAR_Y + (0,):
            for dx in range(NX):
                a = request_id(dx, -dy)
                from_z = jnp.bitwise_and(jnp.right_shift(a, 1), NZ - 1)
                there = jnp.bitwise_and(z - from_z + NZ, NZ - 1)
                piece = gath[there, jnp.bitwise_and(a, 1)]
                if dy == 0:
                    recv2[0, dx] = piece
                else:
                    send2[dy, dx] = piece
            if dy:
                b2.append(remote(send2.at[dy], recv2.at[dy], b2_s.at[dy], b2_r.at[dy], plane(dy, 0)))

    b3 = []

    def along_x():
        for c in b2:
            c.wait_recv()
        for dx in FAR_X + (0,):
            a = request_id(dx, 0)
            from_y = jnp.bitwise_and(jnp.right_shift(a, 4), NY - 1)
            there = jnp.bitwise_and(y - from_y + NY, NY - 1)
            piece = recv2[there, dx]
            if dx == 0:
                recv3[0] = piece
            else:
                send3[dx] = piece
                b3.append(remote(send3.at[dx], recv3.at[dx], b3_s.at[dx], b3_r.at[dx], across(-dx)))

    for dz in (2, 6, 1, 7):
        pass_near(dz)
    attend(1, 0)
    for c in id_y.values():
        c.wait_recv()
    id_z = {dz: remote(col, ids.at[dz], idz_s.at[dz], idz_r.at[dz], plane(0, dz)) for dz in FAR_Z}
    id_x = [remote(col, xids.at[dx], xid_s.at[dx], xid_r.at[dx], across(dx)) for dx in FAR_X]
    attend(1, 1)
    load_a.wait()
    send_group(0)
    pass_on()
    send_group(4)
    send_group(3)
    send_group(5)
    send_group(2)
    send_group(6)
    send_group(1)
    send_group(7)
    along_y()
    attend(2, 0)
    attend(2, 1)
    along_x()
    attend(3, 0)
    attend(3, 1)

    load_t.wait()

    def token_cols(dy, dz):
        owner = lax.rem(y - dy + NY, NY) * NZ + lax.rem(z - dz + NZ, NZ)
        return tok_v[:, pl.ds(pl.multiple_of((owner * 2 + core) * 128, 128), 128)]

    total = jnp.zeros((ROWS, 2 * RANK), jnp.float32)
    for dz in (0,) + FAR_Z:
        some = [(dy, dz) for dy in FAR_Y + (0,)]
        for o in some:
            if o != (0, 0):
                blocks[slot(*o)].wait_recv()
        left = jnp.concatenate([token_cols(*o) for o in some], axis=1)
        right = jnp.concatenate([recv_a[slot(*o)] for o in some], axis=0)
        total = total + jnp.dot(left, right, preferred_element_type=jnp.float32)
    part[...] = total
    swap = remote(part, part_in, p_s, p_r, sibling)
    for c in b3:
        c.wait_recv()
    swap.wait_recv()
    rank = (part[...] + part_in[...]).astype(jnp.bfloat16)

    alive = lax.broadcasted_iota(jnp.int32, (ROWS, HEAD), 0) < live
    for j in range(2):
        whole = jnp.concatenate([recv3[jnp.bitwise_and(x - req + NX, NX - 1), j] for x in range(NX)], axis=0)
        delta = jnp.dot(rank[:, j * RANK:(j + 1) * RANK], whole, preferred_element_type=jnp.float32)
        fresh = base_v[j].astype(jnp.float32) + delta
        for h in range(KV_HEADS):
            one = fresh[:, h * HEAD:(h + 1) * HEAD]
            if j == 0:
                one = one * angle_v[0] + pltpu.roll(one, HEAD // 2, 1) * angle_v[1]
            new_v[j, :, head_cols(h)] = jnp.where(alive, one, 0.0).astype(jnp.bfloat16)
    puts = [pltpu.make_async_copy(new_v, new_out, osem.at[KV_HEADS])]
    puts[0].start()

    column = lax.broadcasted_iota(jnp.int32, (ROWS, HEAD), 1)
    allowed = (column <= row) & (column < live)
    for h in range(KV_HEADS):
        kn = new_v[0, :, head_cols(h)]
        vn = jnp.concatenate([new_v[1, :, head_cols(h)], jnp.ones((ROWS, HEAD), jnp.bfloat16)], axis=1)
        q = jnp.concatenate([q_v[:, head_cols(h * GROUP + i)] for i in range(GROUP)], axis=0)
        s = lax.dot_general(q, kn, (((1,), (1,)), ((), ())), preferred_element_type=jnp.float32)
        s = jnp.where(allowed[None], s.reshape(GROUP, ROWS, HEAD) * SCALE2, LOWEST)
        s = s.reshape(GROUP * ROWS, HEAD)
        r = pl.ds(h * GROUP * ROWS, GROUP * ROWS)
        old = top[r, :]
        m = jnp.maximum(jnp.max(s, axis=1, keepdims=True), old)
        p = jnp.exp2(s - m).astype(jnp.bfloat16)
        o = jnp.dot(p, vn, preferred_element_type=jnp.float32)
        alpha = jnp.exp2(old - m)
        upper = acc[r, 0:HEAD] * alpha + o[:, 0:HEAD]
        lower = acc[r, HEAD:] * alpha + o[:, HEAD:]
        res = upper / lower
        for g in range(GROUP):
            one = jnp.where(alive, res[g * ROWS:(g + 1) * ROWS, :], 0.0)
            out_v[:, head_cols(h * GROUP + g)] = one.astype(jnp.bfloat16)
        cols = pl.ds(h * GROUP * HEAD, GROUP * HEAD)
        c = pltpu.make_async_copy(out_v.at[:, cols], attn_out.at[:, cols], osem.at[h])
        c.start()
        puts.append(c)
    for c in sends:
        c.wait_send()
    for c in puts:
        c.wait()


def write_out(new, attn, new_out, attn_out, new_v, both_v, attn_v, sem, osem):
    loads = [pltpu.make_async_copy(new, new_v, sem.at[KV_HEADS])]
    for h in range(KV_HEADS):
        cols = pl.ds(h * GROUP * HEAD, GROUP * HEAD)
        loads.append(pltpu.make_async_copy(attn.at[:, cols], attn_v.at[:, cols], sem.at[h]))
    for c in loads:
        c.start()
    loads[0].wait()
    both_v[...] = jnp.stack([new_v[0], new_v[1]], axis=1)
    puts = [pltpu.make_async_copy(both_v, new_out, osem.at[KV_HEADS])]
    puts[0].start()
    for h in range(KV_HEADS):
        cols = pl.ds(h * GROUP * HEAD, GROUP * HEAD)
        loads[h + 1].wait()
        puts.append(pltpu.make_async_copy(attn_v.at[:, cols], attn_out.at[:, cols], osem.at[h]))
        puts[-1].start()
    for c in puts:
        c.wait()


def shards(tokens, queries, plain, cached, first, second, adapter, live, ctx):
    width = plain.shape[2]
    bf16, f32 = jnp.bfloat16, jnp.float32
    dma = pltpu.SemaphoreType.DMA
    smem = pl.BlockSpec(memory_space=pltpu.SMEM)
    hbm = pl.BlockSpec(memory_space=pl.ANY)
    heads = KV_HEADS * GROUP
    two = (2, ROWS, width)
    new, attn = pl.pallas_call(
        kernel,
        out_shape=(jax.ShapeDtypeStruct(two, bf16), jax.ShapeDtypeStruct(queries.shape, bf16)),
        in_specs=[smem] * 3 + [hbm] * 6,
        out_specs=(hbm, hbm),
        scratch_shapes=[
            pltpu.VMEM(tokens.shape, bf16),
            pltpu.VMEM(queries.shape, bf16),
            pltpu.VMEM(plain.shape, bf16),
            pltpu.VMEM(two, bf16),
            pltpu.VMEM((2, CTX, width), bf16),
            pltpu.VMEM(first.shape, bf16),
            pltpu.VMEM((PLANE, 128, 2 * RANK), bf16),
            pltpu.VMEM((PLANE, 128, 2 * RANK), bf16),
            pltpu.VMEM((NZ, 2, 2, 16, width), bf16),
            pltpu.VMEM((NY, NX, 2, 16, width), bf16),
            pltpu.VMEM((NY, NX, 2, 16, width), bf16),
            pltpu.VMEM((NX, 2, 16, width), bf16),
            pltpu.VMEM((NX, 2, 16, width), bf16),
            pltpu.VMEM((ROWS, 2 * RANK), f32),
            pltpu.VMEM((ROWS, 2 * RANK), f32),
            pltpu.VMEM((CTX, HEAD), bf16),
            pltpu.VMEM((CTX, 2 * HEAD), bf16),
            pltpu.VMEM((heads * ROWS, 2 * HEAD), f32),
            pltpu.VMEM((heads * ROWS, HEAD), f32),
            pltpu.VMEM((2, ROWS, HEAD), f32),
            pltpu.VMEM(two, bf16),
            pltpu.VMEM(queries.shape, bf16),
            pltpu.SMEM((PLANE, 1), jnp.int32),
            pltpu.SMEM((NZ, PLANE, 1), jnp.int32),
            pltpu.SMEM((NX, PLANE, 1), jnp.int32),
            dma((5,)), dma((KV_HEADS,)), dma((KV_HEADS + 1,)),
            dma((NY,)), dma((NY,)), dma((NZ,)), dma((NZ,)), dma((NX,)), dma((NX,)),
            dma((PLANE,)), dma((PLANE,)), dma((NZ,)), dma((NZ,)),
            dma((NY,)), dma((NY,)), dma((NX,)), dma((NX,)), dma, dma,
        ],
        compiler_params=pltpu.CompilerParams(
            collective_id=0, has_side_effects=True, vmem_limit_bytes=58 << 20
        ),
    )(adapter, live, ctx, tokens, queries, plain, cached, first, second)
    return pl.pallas_call(
        write_out,
        out_shape=(jax.ShapeDtypeStruct(plain.shape, bf16), jax.ShapeDtypeStruct(queries.shape, bf16)),
        in_specs=[hbm, hbm],
        out_specs=(hbm, hbm),
        scratch_shapes=[
            pltpu.VMEM(two, bf16),
            pltpu.VMEM(plain.shape, bf16),
            pltpu.VMEM(queries.shape, bf16),
            dma((KV_HEADS + 1,)),
            dma((KV_HEADS + 1,)),
        ],
        compiler_params=pltpu.CompilerParams(vmem_limit_bytes=58 << 20),
    )(new, attn)


def solution(mesh):
    in_specs = (
        P(("store", "req"), None),
        P(("store", "req"), "tp"),
        P(("store", "req"), None, "tp"),
        P(("store", "req"), None, None, "tp"),
        P(None, ("store", "tp"), None),
        P("store", None, None, "tp"),
        P(("store", "req")),
        P(("store", "req")),
        P(("store", "req")),
    )
    out_specs = (P(("store", "req"), None, "tp"), P(("store", "req"), "tp"))
    return jax.shard_map(shards, mesh=mesh, in_specs=in_specs, out_specs=out_specs, check_vma=False)
```

time: 63.5 us -> 58.8 us (0.926)
  local copies, waits for them, and re-layouts: 4.21 us -> 0 us
    unnamed x2 -> x0, local copies, waits for them, and re-layouts: 4.21 us -> none
    pallas_call x1 -> x2, Pallas kernels: 56.6 us -> 56 us  [the longest x1 53.5 us: shards(): pl.pallas_call(kernel, out_shape=(jax.ShapeDtypeStruct(two, bf16), jax.Sh...]
where the time goes in v2:
time: 58.8 us; the launch traced here: 58.7 us
  Pallas kernels  56 us (95%)
  between operations  2.74 us (5%)
    pallas_call x1, Pallas kernels, shards(): pl.pallas_call(kernel, out_shape=(jax.ShapeDtypeStruct(two, bf16), jax.Sh...  53.5 us
    pallas_call x1, Pallas kernels, shards(): pl.pallas_call(write_out, out_shape=(jax.ShapeDtypeStruct(plain.shape, bf...  2.45 us

profile of v2, /device:TPU:1, one launch (start us, length us, event | category | flops | bytes accessed | tf_op | source)
XLA Modules:
  0.0 58.7 jit_solution(18432099040753784470)
XLA Ops:
  2.6 53.5 %shard_map.104 = (bf16[2,128,512]{2,1,0:T(8,128)(2,1)}, bf16[128,4096]{1,0:T(8,128)(2,1)}) custom-call(s32[1]{0:T(128)S(6)} %copy.11.adapter_ref, s32[1]{0:T(128)S(6)} %copy.12.live_ref, s32[1]{0:T(128)S(6)} %copy.13.ctx_ref, bf16[128,8192]{1,0:T(8,128)(2,1)} %tokens.1, bf16[128,4096]{1,0:T(8,128)(2,1)} %queries.1, bf16[128,2,512]{2,1,0:T(2,128)(2,1)} %plain.1, ...), custom_call_target="tpu_custom_call" | custom-call | tf_op jit(solution)/shard_map/pallas_call | solution.py:324
  56.1 2.5 %shard_map.105 = (bf16[128,2,512]{2,1,0:T(2,128)(2,1)}, bf16[128,4096]{1,0:T(8,128)(2,1)}) custom-call(bf16[2,128,512]{2,1,0:T(8,128)(2,1)} %get-tuple-element.4.new, bf16[128,4096]{1,0:T(8,128)(2,1)} %get-tuple-element.5.attn), custom_call_target="tpu_custom_call" | custom-call | tf_op jit(solution)/shard_map/pallas_call | solution.py:364

commit v3 on v2

--- a/solution.py
+++ b/solution.py
@@ -15,6 +15,7 @@
 PLANE = NY * NZ
 GROUP = 8
 KV_HEADS = 4
+PIECE = 512
 CTX = 2048
 TILE = 512
 SCALE2 = math.log2(math.e) / math.sqrt(HEAD)
@@ -30,15 +31,15 @@
 
 
 def head_cols(h):
-    return pl.ds(h * HEAD, HEAD)
+    return pl.ds(h * HEAD if isinstance(h, int) else pl.multiple_of(h * HEAD, HEAD), HEAD)
 
 
 def kernel(
     adapter_ref, live_ref, ctx_ref, tokens, queries, plain, cached, first, second,
-    new_out, attn_out,
+    new_k, new_w, o0, o1, o2, o3, o4, o5, o6, o7,
     tok_v, q_v, plain_v, base_v, kv_v, first_v, send_a, recv_a, gath, send2, recv2, send3, recv3,
-    part, part_in, key_buf, val_buf, acc, top, angle_v, new_v, out_v, col, ids, xids,
-    lsem, kvsem, osem, idy_s, idy_r, idz_s, idz_r, xid_s, xid_r, a_s, a_r,
+    part, part_in, key_buf, val_buf, acc, top, angle_v, new_v, col, ids, xids,
+    lsem, kvsem, idy_s, idy_r, idz_s, idz_r, xid_s, xid_r, a_s, a_r,
     b1_s, b1_r, b2_s, b2_r, b3_s, b3_r, p_s, p_r,
 ):
     store, req, core = lax.axis_index("store"), lax.axis_index("req"), lax.axis_index("tp")
@@ -91,8 +92,6 @@
     col[0, 0] = adapter_ref[0]
 
     def attend(h, u):
-        if u == 0:
-            prepare(h)
         per = TILE // ROWS
         g = h * GROUP + u * per
         q = jnp.concatenate([q_v[:, head_cols(g + i)] for i in range(per)], axis=0)
@@ -101,13 +100,13 @@
         )
         m = jnp.max(s, axis=1, keepdims=True) * SCALE2
         p = jnp.exp2(s * SCALE2 - m).astype(jnp.bfloat16)
-        r = pl.ds(g * ROWS, TILE)
-        acc[r, :] = jnp.dot(p, val_buf[...], preferred_element_type=jnp.float32)
-        m = jnp.where(ctx > 0, m, LOWEST)
-        top[r, :] = jnp.broadcast_to(m, (TILE, HEAD))
+        o = jnp.dot(p, val_buf[...], preferred_element_type=jnp.float32)
+        lower = jnp.where(ctx > 0, o[:, HEAD:], 1.0)
+        r = pl.ds(pl.multiple_of(g * ROWS, ROWS), TILE)
+        acc[r, :] = o[:, 0:HEAD] / lower
+        top[r, :] = jnp.where(ctx > 0, m + jnp.log2(lower), LOWEST)
 
     def prepare(h):
-        load_kv[h].wait()
         alive = lax.broadcasted_iota(jnp.int32, (CTX, HEAD), 0) < ctx
         k = kv_v[0, :, head_cols(h)]
         v = kv_v[1, :, head_cols(h)]
@@ -115,21 +114,29 @@
         val_buf[:, 0:HEAD] = jnp.where(alive, v, jnp.zeros_like(v))
         val_buf[:, HEAD:] = jnp.where(alive, jnp.ones_like(v), jnp.zeros_like(v))
 
-    load_q.wait()
-    attend(0, 0)
-    attend(0, 1)
-
     lane = lax.broadcasted_iota(jnp.int32, (ROWS, HEAD), 1)
     row = lax.broadcasted_iota(jnp.int32, (ROWS, HEAD), 0)
-    index = jnp.where(lane < HEAD // 2, lane, lane - HEAD // 2).astype(jnp.float32)
-    frequency = jnp.exp(index * (-2.0 / HEAD * math.log(10000.0)))
-    angle = (ctx + row).astype(jnp.float32) * frequency
-    angle_v[0] = jnp.cos(angle)
-    sine = jnp.sin(angle)
-    angle_v[1] = jnp.where(lane < HEAD // 2, -sine, sine)
-    load_p.wait()
-    for j in range(2):
-        base_v[j] = plain_v[:, j, :]
+
+    def attend_heads(lo, hi):
+        for c in load_kv[lo:hi]:
+            c.wait()
+
+        @pl.loop(lo, hi)
+        def _(h):
+            prepare(h)
+            for u in range(GROUP * ROWS // TILE):
+                attend(h, u)
+
+    def angles():
+        index = jnp.where(lane < HEAD // 2, lane, lane - HEAD // 2).astype(jnp.float32)
+        frequency = jnp.exp(index * (-2.0 / HEAD * math.log(10000.0)))
+        angle = (ctx + row).astype(jnp.float32) * frequency
+        angle_v[0] = jnp.cos(angle)
+        sine = jnp.sin(angle)
+        angle_v[1] = jnp.where(lane < HEAD // 2, -sine, sine)
+        load_p.wait()
+        for j in range(2):
+            base_v[j] = plain_v[:, j, :]
 
     pl.semaphore_wait(bar, len(peers))
 
@@ -204,12 +211,12 @@
 
     for dz in (2, 6, 1, 7):
         pass_near(dz)
-    attend(1, 0)
+    load_q.wait()
+    angles()
     for c in id_y.values():
         c.wait_recv()
     id_z = {dz: remote(col, ids.at[dz], idz_s.at[dz], idz_r.at[dz], plane(0, dz)) for dz in FAR_Z}
     id_x = [remote(col, xids.at[dx], xid_s.at[dx], xid_r.at[dx], across(dx)) for dx in FAR_X]
-    attend(1, 1)
     load_a.wait()
     send_group(0)
     pass_on()
@@ -221,11 +228,9 @@
     send_group(1)
     send_group(7)
     along_y()
-    attend(2, 0)
-    attend(2, 1)
+    attend_heads(0, 2)
     along_x()
-    attend(3, 0)
-    attend(3, 1)
+    attend_heads(2, 4)
 
     load_t.wait()
 
@@ -259,8 +264,9 @@
             if j == 0:
                 one = one * angle_v[0] + pltpu.roll(one, HEAD // 2, 1) * angle_v[1]
             new_v[j, :, head_cols(h)] = jnp.where(alive, one, 0.0).astype(jnp.bfloat16)
-    puts = [pltpu.make_async_copy(new_v, new_out, osem.at[KV_HEADS])]
-    puts[0].start()
+    new_k[...] = new_v[0]
+    new_w[...] = new_v[1]
+    outs = (o0, o1, o2, o3, o4, o5, o6, o7)
 
     column = lax.broadcasted_iota(jnp.int32, (ROWS, HEAD), 1)
     allowed = (column <= row) & (column < live)
@@ -277,38 +283,25 @@
         p = jnp.exp2(s - m).astype(jnp.bfloat16)
         o = jnp.dot(p, vn, preferred_element_type=jnp.float32)
         alpha = jnp.exp2(old - m)
-        upper = acc[r, 0:HEAD] * alpha + o[:, 0:HEAD]
-        lower = acc[r, HEAD:] * alpha + o[:, HEAD:]
+        upper = acc[r, :] * alpha + o[:, 0:HEAD]
+        lower = alpha + o[:, HEAD:]
         res = upper / lower
         for g in range(GROUP):
             one = jnp.where(alive, res[g * ROWS:(g + 1) * ROWS, :], 0.0)
-            out_v[:, head_cols(h * GROUP + g)] = one.astype(jnp.bfloat16)
-        cols = pl.ds(h * GROUP * HEAD, GROUP * HEAD)
-        c = pltpu.make_async_copy(out_v.at[:, cols], attn_out.at[:, cols], osem.at[h])
-        c.start()
-        puts.append(c)
+            outs[2 * h + g // 4][:, head_cols(g % 4)] = one.astype(jnp.bfloat16)
     for c in sends:
         c.wait_send()
-    for c in puts:
-        c.wait()
-
-
-def write_out(new, attn, new_out, attn_out, new_v, both_v, attn_v, sem, osem):
-    loads = [pltpu.make_async_copy(new, new_v, sem.at[KV_HEADS])]
-    for h in range(KV_HEADS):
-        cols = pl.ds(h * GROUP * HEAD, GROUP * HEAD)
-        loads.append(pltpu.make_async_copy(attn.at[:, cols], attn_v.at[:, cols], sem.at[h]))
-    for c in loads:
-        c.start()
-    loads[0].wait()
-    both_v[...] = jnp.stack([new_v[0], new_v[1]], axis=1)
-    puts = [pltpu.make_async_copy(both_v, new_out, osem.at[KV_HEADS])]
-    puts[0].start()
-    for h in range(KV_HEADS):
-        cols = pl.ds(h * GROUP * HEAD, GROUP * HEAD)
-        loads[h + 1].wait()
-        puts.append(pltpu.make_async_copy(attn_v.at[:, cols], attn_out.at[:, cols], osem.at[h]))
+
+
+def write_out(new_k, new_w, o0, o1, o2, o3, o4, o5, o6, o7, new_out, attn_out, both_v, sem):
+    puts = []
+    for i, part in enumerate((o0, o1, o2, o3, o4, o5, o6, o7)):
+        cols = pl.ds(i * PIECE, PIECE)
+        puts.append(pltpu.make_async_copy(part, attn_out.at[:, cols], sem.at[i]))
         puts[-1].start()
+    both_v[...] = jnp.stack([new_k[...], new_w[...]], axis=1)
+    puts.append(pltpu.make_async_copy(both_v, new_out, sem.at[8]))
+    puts[-1].start()
     for c in puts:
         c.wait()
 
@@ -319,13 +312,14 @@
     dma = pltpu.SemaphoreType.DMA
     smem = pl.BlockSpec(memory_space=pltpu.SMEM)
     hbm = pl.BlockSpec(memory_space=pl.ANY)
+    vmem = pl.BlockSpec(memory_space=pltpu.VMEM)
     heads = KV_HEADS * GROUP
     two = (2, ROWS, width)
-    new, attn = pl.pallas_call(
+    pieces = pl.pallas_call(
         kernel,
-        out_shape=(jax.ShapeDtypeStruct(two, bf16), jax.ShapeDtypeStruct(queries.shape, bf16)),
+        out_shape=(jax.ShapeDtypeStruct((ROWS, PIECE), bf16),) * 10,
         in_specs=[smem] * 3 + [hbm] * 6,
-        out_specs=(hbm, hbm),
+        out_specs=(vmem,) * 10,
         scratch_shapes=[
             pltpu.VMEM(tokens.shape, bf16),
             pltpu.VMEM(queries.shape, bf16),
@@ -344,37 +338,30 @@
             pltpu.VMEM((ROWS, 2 * RANK), f32),
             pltpu.VMEM((CTX, HEAD), bf16),
             pltpu.VMEM((CTX, 2 * HEAD), bf16),
-            pltpu.VMEM((heads * ROWS, 2 * HEAD), f32),
+            pltpu.VMEM((heads * ROWS, HEAD), f32),
             pltpu.VMEM((heads * ROWS, HEAD), f32),
             pltpu.VMEM((2, ROWS, HEAD), f32),
             pltpu.VMEM(two, bf16),
-            pltpu.VMEM(queries.shape, bf16),
             pltpu.SMEM((PLANE, 1), jnp.int32),
             pltpu.SMEM((NZ, PLANE, 1), jnp.int32),
             pltpu.SMEM((NX, PLANE, 1), jnp.int32),
-            dma((5,)), dma((KV_HEADS,)), dma((KV_HEADS + 1,)),
+            dma((5,)), dma((KV_HEADS,)),
             dma((NY,)), dma((NY,)), dma((NZ,)), dma((NZ,)), dma((NX,)), dma((NX,)),
             dma((PLANE,)), dma((PLANE,)), dma((NZ,)), dma((NZ,)),
             dma((NY,)), dma((NY,)), dma((NX,)), dma((NX,)), dma, dma,
         ],
         compiler_params=pltpu.CompilerParams(
-            collective_id=0, has_side_effects=True, vmem_limit_bytes=58 << 20
+            collective_id=0, has_side_effects=True, vmem_limit_bytes=105 << 19
         ),
     )(adapter, live, ctx, tokens, queries, plain, cached, first, second)
     return pl.pallas_call(
         write_out,
         out_shape=(jax.ShapeDtypeStruct(plain.shape, bf16), jax.ShapeDtypeStruct(queries.shape, bf16)),
-        in_specs=[hbm, hbm],
+        in_specs=[vmem] * 10,
         out_specs=(hbm, hbm),
-        scratch_shapes=[
-            pltpu.VMEM(two, bf16),
-            pltpu.VMEM(plain.shape, bf16),
-            pltpu.VMEM(queries.shape, bf16),
-            dma((KV_HEADS + 1,)),
-            dma((KV_HEADS + 1,)),
-        ],
-        compiler_params=pltpu.CompilerParams(vmem_limit_bytes=58 << 20),
-    )(new, attn)
+        scratch_shapes=[pltpu.VMEM(plain.shape, bf16), dma((9,))],
+        compiler_params=pltpu.CompilerParams(vmem_limit_bytes=8 << 20),
+    )(*pieces)
 
 
 def solution(mesh):

time: 58.8 us -> 56 us (0.952)
  Pallas kernels: 56 us -> 53.1 us
    pallas_call x1, Pallas kernels: 53.5 us -> 51.9 us  [shards(): pl.pallas_call(kernel, out_shape=(jax.ShapeDtypeStruct((ROWS, PIECE), bf1...]
    pallas_call x1, Pallas kernels: 2.45 us -> 1.15 us  [shards(): pl.pallas_call(write_out, out_shape=(jax.ShapeDtypeStruct(plain.shape, bf...]
where the time goes in v3:
time: 56 us; the launch traced here: 55.6 us
  Pallas kernels  53.1 us (95%)
  between operations  2.58 us (5%)
    pallas_call x1, Pallas kernels, shards(): pl.pallas_call(kernel, out_shape=(jax.ShapeDtypeStruct((ROWS, PIECE), bf1...  51.9 us
    pallas_call x1, Pallas kernels, shards(): pl.pallas_call(write_out, out_shape=(jax.ShapeDtypeStruct(plain.shape, bf...  1.15 us

profile of v3, /device:TPU:1, one launch (start us, length us, event | category | flops | bytes accessed | tf_op | source)
XLA Modules:
  0.0 55.6 jit_solution(14584740280203417750)
XLA Ops:
  2.6 51.9 %shard_map.104 = (bf16[128,512]{1,0:T(8,128)(2,1)S(1)}, bf16[128,512]{1,0:T(8,128)(2,1)S(1)}, bf16[128,512]{1,0:T(8,128)(2,1)S(1)}, bf16[128,512]{1,0:T(8,128)(2...) custom-call(s32[1]{0:T(128)S(6)} %copy.11.adapter_ref, ...), custom_call_target="tpu_custom_call" | custom-call | tf_op jit(solution)/shard_map/pallas_call | solution.py:318
  54.5 1.2 %shard_map.105 = (bf16[128,2,512]{2,1,0:T(2,128)(2,1)}, bf16[128,4096]{1,0:T(8,128)(2,1)}) custom-call(bf16[128,512]{1,0:T(8,128)(2,1)S(1)} %get-tuple-element.12.new_k, bf16[128,512]{1,0:T(8,128)(2,1)S(1)} %get-tuple-element.13.new_w, bf16[128,512]{1,0:T(8,128)(2,1)S(1)} %get-tuple-element.14.o0, bf16[128,512]{1,0:T(8,128)(2,1)S(1)} %get-tuple-element.15.o1, ...), custom_call_target="tpu_custom_call" | custom-call | tf_op jit(solution)/shard_map/pallas_call | solution.py:357

commit v4 on v3

--- a/solution.py
+++ b/solution.py
@@ -220,13 +220,13 @@
     load_a.wait()
     send_group(0)
     pass_on()
-    send_group(4)
+    send_group(1)
+    send_group(7)
+    send_group(2)
+    send_group(6)
     send_group(3)
     send_group(5)
-    send_group(2)
-    send_group(6)
-    send_group(1)
-    send_group(7)
+    send_group(4)
     along_y()
     attend_heads(0, 2)
     along_x()

time: 56 us -> 53.8 us (0.961)
  Pallas kernels: 53.1 us -> 51 us
    pallas_call x1, Pallas kernels: 51.9 us -> 49.8 us  [shards(): pl.pallas_call(kernel, out_shape=(jax.ShapeDtypeStruct((ROWS, PIECE), bf1...]
where the time goes in v4:
time: 53.8 us; the launch traced here: 53.5 us
  Pallas kernels  51 us (95%)
  between operations  2.58 us (5%)
    pallas_call x1, Pallas kernels, shards(): pl.pallas_call(kernel, out_shape=(jax.ShapeDtypeStruct((ROWS, PIECE), bf1...  49.8 us
    pallas_call x1, Pallas kernels, shards(): pl.pallas_call(write_out, out_shape=(jax.ShapeDtypeStruct(plain.shape, bf...  1.15 us

profile of v4, /device:TPU:1, one launch (start us, length us, event | category | flops | bytes accessed | tf_op | source)
XLA Modules:
  0.0 53.5 jit_solution(1916460252431582938)
XLA Ops:
  2.6 49.8 %shard_map.104 = (bf16[128,512]{1,0:T(8,128)(2,1)S(1)}, bf16[128,512]{1,0:T(8,128)(2,1)S(1)}, bf16[128,512]{1,0:T(8,128)(2,1)S(1)}, bf16[128,512]{1,0:T(8,128)(2...) custom-call(s32[1]{0:T(128)S(6)} %copy.11.adapter_ref, ...), custom_call_target="tpu_custom_call" | custom-call | tf_op jit(solution)/shard_map/pallas_call | solution.py:318
  52.4 1.2 %shard_map.105 = (bf16[128,2,512]{2,1,0:T(2,128)(2,1)}, bf16[128,4096]{1,0:T(8,128)(2,1)}) custom-call(bf16[128,512]{1,0:T(8,128)(2,1)S(1)} %get-tuple-element.12.new_k, bf16[128,512]{1,0:T(8,128)(2,1)S(1)} %get-tuple-element.13.new_w, bf16[128,512]{1,0:T(8,128)(2,1)S(1)} %get-tuple-element.14.o0, bf16[128,512]{1,0:T(8,128)(2,1)S(1)} %get-tuple-element.15.o1, ...), custom_call_target="tpu_custom_call" | custom-call | tf_op jit(solution)/shard_map/pallas_call | solution.py:357

commit v5 on v4

--- a/solution.py
+++ b/solution.py
@@ -23,6 +23,7 @@
 FAR_X = (2, 1, 3)
 FAR_Y = (2, 1, 3)
 FAR_Z = (4, 3, 5, 2, 6, 1, 7)
+NEAR_Z = (1, 7, 2, 6, 3, 5, 4)
 REST = (1, 7, 3, 5, 4, 0)
 MESH = pl.DeviceIdType.MESH
 
@@ -220,13 +221,8 @@
     load_a.wait()
     send_group(0)
     pass_on()
-    send_group(1)
-    send_group(7)
-    send_group(2)
-    send_group(6)
-    send_group(3)
-    send_group(5)
-    send_group(4)
+    for dz in NEAR_Z:
+        send_group(dz)
     along_y()
     attend_heads(0, 2)
     along_x()
@@ -239,7 +235,7 @@
         return tok_v[:, pl.ds(pl.multiple_of((owner * 2 + core) * 128, 128), 128)]
 
     total = jnp.zeros((ROWS, 2 * RANK), jnp.float32)
-    for dz in (0,) + FAR_Z:
+    for dz in (0,) + NEAR_Z:
         some = [(dy, dz) for dy in FAR_Y + (0,)]
         for o in some:
             if o != (0, 0):

time: 53.8 us -> 52.7 us (0.980)
  Pallas kernels: 51 us -> 49.8 us
    pallas_call x1, Pallas kernels: 49.8 us -> 48.7 us  [shards(): pl.pallas_call(kernel, out_shape=(jax.ShapeDtypeStruct((ROWS, PIECE), bf1...]
where the time goes in v5:
time: 52.7 us; the launch traced here: 52.4 us
  Pallas kernels  49.8 us (94%)
  between operations  2.58 us (5%)
    pallas_call x1, Pallas kernels, shards(): pl.pallas_call(kernel, out_shape=(jax.ShapeDtypeStruct((ROWS, PIECE), bf1...  48.7 us
    pallas_call x1, Pallas kernels, shards(): pl.pallas_call(write_out, out_shape=(jax.ShapeDtypeStruct(plain.shape, bf...  1.15 us

profile of v5, /device:TPU:1, one launch (start us, length us, event | category | flops | bytes accessed | tf_op | source)
XLA Modules:
  0.0 52.4 jit_solution(4367136466005249497)
XLA Ops:
  2.6 48.7 %shard_map.104 = (bf16[128,512]{1,0:T(8,128)(2,1)S(1)}, bf16[128,512]{1,0:T(8,128)(2,1)S(1)}, bf16[128,512]{1,0:T(8,128)(2,1)S(1)}, bf16[128,512]{1,0:T(8,128)(2...) custom-call(s32[1]{0:T(128)S(6)} %copy.11.adapter_ref, ...), custom_call_target="tpu_custom_call" | custom-call | tf_op jit(solution)/shard_map/pallas_call | solution.py:314
  51.2 1.2 %shard_map.105 = (bf16[128,2,512]{2,1,0:T(2,128)(2,1)}, bf16[128,4096]{1,0:T(8,128)(2,1)}) custom-call(bf16[128,512]{1,0:T(8,128)(2,1)S(1)} %get-tuple-element.12.new_k, bf16[128,512]{1,0:T(8,128)(2,1)S(1)} %get-tuple-element.13.new_w, bf16[128,512]{1,0:T(8,128)(2,1)S(1)} %get-tuple-element.14.o0, bf16[128,512]{1,0:T(8,128)(2,1)S(1)} %get-tuple-element.15.o1, ...), custom_call_target="tpu_custom_call" | custom-call | tf_op jit(solution)/shard_map/pallas_call | solution.py:353
